TPU v7x, 32 devices: a whole 2x2x4 slice. The times are simulated.
32 devices in a mesh: groups: 2 (over y), pool: 4 (over z), tp: 4 (over x, core).
Axes of the slice: x: 2, y: 2, z: 4, core: 2. Of those that a mesh axis runs over, the one named last changes fastest.
Arguments:
- tokens: bfloat16 [2560, 8192], P(('groups', 'pool'), 'tp'), parts along dimension 0, may hold values from -6 to 6
- w_kv: bfloat16 [8192, 8, 256], P('tp'), may hold values from -0.0625 to 0.0625
- prompt_lens: int32 [32], P('groups'), parts along dimension 0, may hold values from 1 to 640, 1280 in all
- routes: int32 [320, 1], P('groups'), parts along dimension 0, may hold values from 0 to 3; in each aligned block of 40 rows (0 to 39, 40 to 79, ...) at most 20 rows name the same one
Outputs:
- handed: bfloat16 [8, 4, 20, 8, 8, 256], P(('groups', 'pool'), None, None, None, 'tp'), parts along dimension 0
There are 2 independent parts, one for each index of `groups`. A program takes and returns all parts, laid end to end along the dimension named above; an argument that names none is the same for every part. Nothing has to cross between parts.
Inputs may be any that keep to these rules, and one draw needn't show every extreme that they name: `routes`: each pool index's 40 pages name every destination at most 20 times.
All inputs are finite; a program needn't handle non-finite values.
Results may differ from a plain program's by a relative error of at most 0.001.
Values may be sent and summed in bfloat16 or wider, within the bound.
A program may use at most 64 MiB of HBM per device.

v0:
```python
import math

import jax
import jax.numpy as jnp
from jax import lax
from jax.sharding import PartitionSpec as P

BLOCK = 8


def frequencies(head_dim):
    half = head_dim // 2
    base = jnp.exp(
        jnp.arange(half, dtype=jnp.float32) * (-2.0 / head_dim) * jnp.log(jnp.float32(500000.0))
    )
    wavelength = 2.0 * math.pi / base
    smooth = (8192.0 / wavelength - 1.0) / 3.0
    middle = (1.0 - smooth) * base / 8.0 + smooth * base
    return jnp.where(wavelength < 2048.0, base, jnp.where(wavelength > 8192.0, base / 8.0, middle))


def rotate(key_rows, positions):
    half = key_rows.shape[-1] // 2
    freqs = frequencies(key_rows.shape[-1])
    angle = positions.astype(jnp.float32)[:, None] * freqs[None, :]
    cosine = jnp.cos(angle)[:, None, :]
    sine = jnp.sin(angle)[:, None, :]
    first = key_rows[..., :half]
    second = key_rows[..., half:]
    return jnp.concatenate(
        [first * cosine - second * sine, second * cosine + first * sine], axis=-1
    )


def ranks_of(targets, width):
    matches = (targets[..., None] == jnp.arange(width, dtype=jnp.int32)).astype(jnp.int32)
    return jnp.sum((jnp.cumsum(matches, axis=-2) - matches) * matches, axis=-1)


def on_device(tokens, w_kv, prompt_lens, routes):
    pool_index = lax.axis_index("pool")
    pool_size = lax.axis_size("pool")
    tp_size = lax.axis_size("tp")
    pre_tok = tokens.shape[0]
    all_heads = w_kv.shape[1]
    local_heads = all_heads // tp_size
    head_dim = w_kv.shape[2] // 2
    page_count = pre_tok // BLOCK
    most = max(2, 2 * page_count // pool_size)
    summed = lax.psum_scatter(
        jnp.einsum("td,dkc->ktc", tokens, w_kv, preferred_element_type=jnp.float32),
        "tp",
        scatter_dimension=0,
        tiled=True,
    )
    kv_rows = jnp.transpose(summed, (1, 0, 2))
    token_index = pool_index * pre_tok + jnp.arange(pre_tok, dtype=jnp.int32)
    prompt_ends = jnp.cumsum(prompt_lens)
    before = jnp.sum(
        jnp.where(prompt_ends[None, :] <= token_index[:, None], prompt_lens[None, :], 0), axis=1
    )
    positions = token_index - before
    rotated = rotate(kv_rows[..., :head_dim], positions)
    pages = jnp.concatenate([rotated, kv_rows[..., head_dim:]], axis=-1).astype(jnp.bfloat16)
    pages = pages.reshape(page_count, BLOCK, local_heads, 2 * head_dim)
    slot_count = pool_size * most
    all_targets = routes[:, 0]
    every_page = lax.all_gather(pages, "pool", axis=0, tiled=True)
    target_grid = all_targets.reshape(pool_size, page_count)
    ranking = ranks_of(target_grid, pool_size).reshape(pool_size * page_count)
    sources = jnp.arange(pool_size * page_count, dtype=jnp.int32) // page_count
    slot_ids = sources * most + ranking
    picked = (all_targets[:, None] == pool_index) & (
        slot_ids[:, None] == jnp.arange(slot_count, dtype=jnp.int32)[None, :]
    )
    placed = jnp.dot(
        picked.astype(jnp.bfloat16).T,
        every_page.reshape(pool_size * page_count, -1),
        preferred_element_type=jnp.float32,
    )
    received = placed.astype(jnp.bfloat16).reshape(
        pool_size, most, BLOCK, local_heads, 2 * head_dim
    )
    return received[None]


def solution(mesh):
    placed = (P(("groups", "pool"), "tp"), P("tp", None, None), P("groups"), P("groups", None))
    return jax.shard_map(
        on_device,
        mesh=mesh,
        in_specs=placed,
        out_specs=P(("groups", "pool"), None, None, None, "tp", None),
        check_vma=False,
    )
```

profile of v0, /device:TPU:0, one launch (start us, length us, event | category | flops | bytes accessed | tf_op | source)
XLA Modules:
  0.0 104.9 jit_solution(12906450116989238569)
XLA Ops:
  6.5 1.3 %copy-done = bf16[320,2048]{1,0:T(8,128)(2,1)S(1)} copy-done((bf16[320,2048]{1,0:T(8,128)(2,1)S(1)}, bf16[320,2048]{1,0:T(8,128)(2,1)}, u32[]{:S(2)}) %copy-start) | copy-done | bytes 1310744
  7.9 7.8 %fusion.2 = f32[8,320,256]{2,1,0:T(8,128)} fusion(bf16[2048,8,256]{2,1,0:T(8,128)(2,1)} %param.5, bf16[320,2048]{1,0:T(8,128)(2,1)S(1)} %copy-done), kind=kOutput, calls=%fused_computation.3 | convolution fusion | flops 2684354560 | bytes 12320768 | tf_op jit(solution)/shard_map/td,dkc->ktc/dot_general | solution.py:51
  15.7 0.6 copy-done.2
  16.3 0.1 copy.19
  16.4 0.1 reduce.2
  16.6 0.1 select_reduce_fusion.1
  16.7 0.6 multiply_cosine_fusion
  17.3 35.8 %reduce-scatter.2.cloned.1.call-done = f32[2,320,256]{2,1,0:T(8,128)} async-done(((f32[8,320,256]{2,1,0:T(8,128)}), f32[2,320,256]{2,1,0:T(8,128)}) %reduce-scatter.2.cloned.1.call-update) | async-done | bytes 655376 | tf_op jit(solution)/shard_map/reduce_scatter | solution.py:50
  53.2 1.0 fusion.8
  54.2 1.3 %fusion.6 = (bf16[40,8,2,64]{3,1,0,2:T(8,128)(2,1)S(1)}, bf16[40,8,2,64]{3,1,0,2:T(8,128)(2,1)S(1)}) fusion(f32[320,2,256]{2,0,1:T(8,128)} %bitcast.16, f32[320,64]{1,0:T(8,128)S(1)} %get-tuple-element.8, f32[320,64]{1,0:T(8,128)S(1)} %get-tuple-element.7), kind=kLoop, calls=%fused_computation.11 | loop fusion | flops 327680 | bytes 655360 | tf_op jit(solution)/shard_map/concatenate | solution.py:64
  55.4 0.2 pad_maximum_fusion
  55.6 0.7 copy.24
  56.4 0.5 broadcast.142
  56.9 0.6 reduce.6
  57.6 0.1 eq.36
  57.7 0.1 fusion.9
  57.8 0.1 reduce_window_sum.18
  57.9 0.2 select_reduce_fusion
  58.1 0.1 reshape.135
  58.2 31.0 %all-gather.2.cloned.1.call-done = bf16[160,8,2,256]{3,1,2,0:T(8,128)(2,1)} async-done(((bf16[40,8,2,256]{3,1,2,0:T(8,128)(2,1)}), bf16[160,8,2,256]{3,1,2,0:T(8,128)(2,1)}) %all-gather.2.cloned.1.call-update) | async-done | bytes 1310736 | tf_op jit(solution)/shard_map/all_gather | solution.py:68
  89.2 3.7 %copy.23 = bf16[160,8,2,256]{3,2,1,0:T(2,128)(2,1)} copy(bf16[160,8,2,256]{3,1,2,0:T(8,128)(2,1)} %all-gather.2.cloned.1.call-done) | data formatting | bytes 2621440 | tf_op jit(solution)/shard_map/all_gather | solution.py:68
  92.9 3.4 %reshape.138 = bf16[160,4096]{1,0:T(8,128)(2,1)S(1)} reshape(bf16[160,8,2,256]{3,2,1,0:T(2,128)(2,1)} %copy.23) | data formatting | bytes 2621440 | tf_op jit(solution)/shard_map/reshape | solution.py:78
  96.3 0.5 convolution_convert_fusion
  96.8 1.3 %broadcast_in_dim_reshape.3 = bf16[1,4,20,8,2,256]{5,4,3,2,1,0:T(2,128)(2,1)} reshape(bf16[80,4096]{1,0:T(8,128)(2,1)S(1)} %convolution_convert_fusion) | data formatting | bytes 1310720 | tf_op jit(solution)/shard_map/broadcast_in_dim;reshape | solution.py:84
  (14 shorter events, 0.2 us)
Async XLA Ops:
  6.5 1.3 %copy-start = (bf16[320,2048]{1,0:T(8,128)(2,1)S(1)}, bf16[320,2048]{1,0:T(8,128)(2,1)}, u32[]{:S(2)}) copy-start(bf16[320,2048]{1,0:T(8,128)(2,1)} %param.4) | copy-start | bytes 3932164
  6.5 46.6 %reduce-scatter.2.cloned.1.call-start = ((), (), s32[]{:S(2)}) async-start(), calls=%async_computation.1 | async-start | bytes 3276800 | tf_op jit(solution)/shard_map/reduce_scatter | solution.py:50
  15.6 0.7 copy-start.2
  15.7 73.6 %all-gather.2.cloned.1.call-start = ((), (), s32[]{:S(2)}) async-start(), calls=%async_computation.2 | async-start | bytes 1638400 | tf_op jit(solution)/shard_map/all_gather | solution.py:68
  54.2 2.8 %copy-start.1 = (s32[160,1]{0,1:T(1,128)S(1)}, s32[160,1]{0,1:T(1,128)}, u32[]{:S(2)}) copy-start(s32[160,1]{0,1:T(1,128)} %param.7) | copy-start | bytes 1924
Sparse Core Ops, SparseCore 0:
  15.8 37.3 reduce-scatter.1
  56.5 32.6 all-gather.1
where the time goes:
time: 105 us
  waiting for transfers between devices  66.9 us (64%)
  between operations  13.5 us (13%)
  local copies, waits for them, and re-layouts  12.8 us (12%)
  matrix products  8.24 us (8%)
  other arithmetic  3.42 us (3%)
    reduce_scatter x1, waiting for transfers between devices, on_device(): lax.psum_scatter(jnp.einsum('td,dkc->ktc', tokens, w_kv, preferred_elemen...  35.8 us
    all_gather x1, waiting for transfers between devices, on_device(): every_page = lax.all_gather(pages, 'pool', axis=0, tiled=True)  31 us
    dot_general x1, matrix products, on_device(): jnp.einsum('td,dkc->ktc', tokens, w_kv, preferred_element_type=jnp.float32)  7.78 us
    all_gather x1, local copies, waits for them, and re-layouts, on_device(): every_page = lax.all_gather(pages, 'pool', axis=0, tiled=True)  3.67 us
    reshape x1, local copies, waits for them, and re-layouts, on_device(): every_page.reshape(pool_size * page_count, -1)  3.38 us
    unnamed x7, local copies, waits for them, and re-layouts  2.44 us
  transfers between devices with their start and end apart: 2, of which 2 were waited for; matrix products, arithmetic and copies ran while one was open for 3% of the time, Pallas kernels for 0%

commit v1 on v0

v1 whole, which is shorter than its diff:
```python
import functools
import math

import jax
import jax.numpy as jnp
from jax import lax
from jax.experimental import pallas as pl
from jax.experimental.pallas import tpu as pltpu
from jax.sharding import PartitionSpec as P

BLOCK = 8
LANES = 128
MESH = pl.DeviceIdType.MESH


def frequencies(head_dim):
    half = head_dim // 2
    base = jnp.exp(
        jnp.arange(half, dtype=jnp.float32) * (-2.0 / head_dim) * jnp.log(jnp.float32(500000.0))
    )
    wavelength = 2.0 * math.pi / base
    smooth = (8192.0 / wavelength - 1.0) / 3.0
    middle = (1.0 - smooth) * base / 8.0 + smooth * base
    return jnp.where(wavelength < 2048.0, base, jnp.where(wavelength > 8192.0, base / 8.0, middle))


def hand_over(
    pool_size, tp_size, most,
    partial_ref, freq_ref, lens_row_ref, lens_col_ref, route_row_ref, route_col_ref,
    out_ref,
    pair_in, across_out, across_in, placed, select, cosine, sine,
    pair_sems, across_sems, pool_sems, local_sems,
):
    pool_index = lax.axis_index("pool")
    tp_index = lax.axis_index("tp")
    chip, core = tp_index // 2, tp_index % 2
    chips = tp_size // 2
    rows = partial_ref.shape[1]
    local_heads = partial_ref.shape[0] // tp_size
    parts = partial_ref.shape[2] // LANES
    chunks = [(j, part) for j in range(local_heads) for part in range(parts)]
    span = most * BLOCK
    page_count = rows // BLOCK
    slot_rows = pool_size * span

    def head_of(chip_of, core_of, j):
        return (chip_of * 2 + core_of) * local_heads + j

    barrier = pltpu.get_barrier_semaphore()
    peers = [{"tp": chip * 2 + 1 - core}]
    peers += [{"tp": lax.rem(chip + d, chips) * 2 + core} for d in range(1, chips)]
    peers += [{"pool": lax.rem(pool_index + d, pool_size)} for d in range(1, pool_size)]
    for peer in peers:
        pl.semaphore_signal(barrier, inc=1, device_id=peer, device_id_type=MESH)
    pl.semaphore_wait(barrier, len(peers))

    def window(head, part):
        return partial_ref.at[head, :, pl.ds(part * LANES, LANES)]

    def pair_copy(n, d):
        j, part = chunks[n]
        return pltpu.make_async_remote_copy(
            src_ref=window(head_of(lax.rem(chip + d, chips), 1 - core, j), part),
            dst_ref=pair_in.at[n, d],
            send_sem=pair_sems.at[0, n, d],
            recv_sem=pair_sems.at[1, n, d],
            device_id={"tp": chip * 2 + 1 - core},
            device_id_type=MESH,
        )

    def across_copy(n, d):
        return pltpu.make_async_remote_copy(
            src_ref=across_out.at[n, d - 1],
            dst_ref=across_in.at[n, d - 1],
            send_sem=across_sems.at[0, n, d - 1],
            recv_sem=across_sems.at[1, n, d - 1],
            device_id={"tp": lax.rem(chip + d, chips) * 2 + core},
            device_id_type=MESH,
        )

    def pool_copy(n, d):
        target = lax.rem(pool_index + d, pool_size)
        return pltpu.make_async_remote_copy(
            src_ref=placed.at[n, pl.ds(pl.multiple_of(target * span, span), span)],
            dst_ref=out_ref.at[
                pl.ds(pl.multiple_of(pool_index * span, span), span), pl.ds(n * LANES, LANES)
            ],
            send_sem=pool_sems.at[0, n, d - 1],
            recv_sem=pool_sems.at[1, n, d - 1],
            device_id={"pool": target},
            device_id_type=MESH,
        )

    def own_copy(n):
        block = pl.ds(pl.multiple_of(pool_index * span, span), span)
        return pltpu.make_async_copy(
            placed.at[n, block], out_ref.at[block, pl.ds(n * LANES, LANES)], local_sems.at[n]
        )

    hops = [d % chips for d in range(1, chips + 1)]
    for n in range(len(chunks)):
        for d in hops:
            pair_copy(n, d).start()
    for n, (j, part) in enumerate(chunks):
        for d in range(1, chips):
            pair_copy(n, d).wait_recv()
            head = head_of(lax.rem(chip + d, chips), core, j)
            across_out[n, d - 1] = (
                partial_ref[head, :, part * LANES:(part + 1) * LANES] + pair_in[n, d]
            )
            across_copy(n, d).start()

    def iota(shape, axis):
        return lax.broadcasted_iota(jnp.int32, shape, axis)

    prompts = lens_row_ref.shape[1]
    upto = iota((prompts, prompts), 0) <= iota((prompts, prompts), 1)
    ends = jnp.sum(jnp.where(upto, lens_col_ref[...].astype(jnp.float32), 0.0), axis=0, keepdims=True)
    token = (pool_index * rows + iota((rows, prompts), 0)).astype(jnp.float32)
    before = jnp.sum(
        jnp.where(ends <= token, lens_row_ref[...].astype(jnp.float32), 0.0), axis=1, keepdims=True
    )
    position = token[:, :1] - before
    angle = position * freq_ref[...]
    cosine[...] = jnp.cos(angle)
    turned = jnp.sin(angle)
    sine[...] = jnp.where(iota((rows, LANES), 1) < LANES // 2, -turned, turned)

    pages = route_row_ref.shape[1]
    first = pool_index * page_count
    target_row = jnp.sum(
        jnp.where(
            iota((pages, rows), 0) == first + (iota((pages, rows), 1) >> 3),
            route_col_ref[...].astype(jnp.float32),
            0.0,
        ),
        axis=0,
        keepdims=True,
    )
    target_col = jnp.sum(
        jnp.where(
            iota((rows, pages), 1) == first + (iota((rows, pages), 0) >> 3),
            route_row_ref[...].astype(jnp.float32),
            0.0,
        ),
        axis=1,
        keepdims=True,
    )
    earlier = (iota((rows, rows), 0) >> 3) < (iota((rows, rows), 1) >> 3)
    rank = jnp.sum(
        jnp.where(earlier & (target_col == target_row), 1.0, 0.0), axis=0, keepdims=True
    )
    slot = target_row * span + rank + (iota((1, rows), 1) & 7).astype(jnp.float32)
    select[...] = jnp.where(
        iota((slot_rows, rows), 0).astype(jnp.float32) == slot, 1.0, 0.0
    ).astype(jnp.bfloat16)

    for n, (j, part) in enumerate(chunks):
        pair_copy(n, 0).wait_recv()
        total = (
            partial_ref[head_of(chip, core, j), :, part * LANES:(part + 1) * LANES] + pair_in[n, 0]
        )
        for d in range(1, chips):
            across_copy(n, d).wait_recv()
            total = total + across_in[n, d - 1]
        if part == 0:
            half = LANES // 2
            swapped = jnp.concatenate([total[:, half:], total[:, :half]], axis=1)
            total = total * cosine[...] + swapped * sine[...]
        placed[n] = jnp.dot(
            select[...], total.astype(jnp.bfloat16), preferred_element_type=jnp.float32
        ).astype(jnp.bfloat16)
        for d in range(1, pool_size):
            pool_copy(n, d).start()
        own_copy(n).start()

    for n in range(len(chunks)):
        own_copy(n).wait()
        for d in range(chips):
            pair_copy(n, d).wait_send()
        for d in range(1, chips):
            across_copy(n, d).wait_send()
        for d in range(1, pool_size):
            pool_copy(n, d).wait()


def on_device(pool_size, tp_size, tokens, w_kv, prompt_lens, routes):
    rows = tokens.shape[0]
    heads, width = w_kv.shape[1:]
    local_heads = heads // tp_size
    most = max(2, 2 * (rows // BLOCK) // pool_size)
    slot_rows = pool_size * most * BLOCK
    partial = jnp.einsum("td,dkc->ktc", tokens, w_kv, preferred_element_type=jnp.float32)
    freqs = frequencies(width // 2)
    chunks = local_heads * width // LANES
    chips = tp_size // 2
    vmem = pl.BlockSpec(memory_space=pltpu.VMEM)
    received = pl.pallas_call(
        functools.partial(hand_over, pool_size, tp_size, most),
        out_shape=jax.ShapeDtypeStruct((slot_rows, local_heads * width), jnp.bfloat16),
        in_specs=[vmem] * 6,
        out_specs=vmem,
        scratch_shapes=[
            pltpu.VMEM((chunks, chips, rows, LANES), jnp.float32),
            pltpu.VMEM((chunks, chips - 1, rows, LANES), jnp.float32),
            pltpu.VMEM((chunks, chips - 1, rows, LANES), jnp.float32),
            pltpu.VMEM((chunks, slot_rows, LANES), jnp.bfloat16),
            pltpu.VMEM((slot_rows, rows), jnp.bfloat16),
            pltpu.VMEM((rows, LANES), jnp.float32),
            pltpu.VMEM((rows, LANES), jnp.float32),
            pltpu.SemaphoreType.DMA((2, chunks, chips)),
            pltpu.SemaphoreType.DMA((2, chunks, chips - 1)),
            pltpu.SemaphoreType.DMA((2, chunks, pool_size - 1)),
            pltpu.SemaphoreType.DMA((chunks,)),
        ],
        compiler_params=pltpu.CompilerParams(
            collective_id=0, has_side_effects=True, vmem_limit_bytes=40 * 2**20
        ),
    )(
        partial,
        jnp.concatenate([freqs, freqs])[None, :],
        prompt_lens[None, :],
        prompt_lens[:, None],
        routes.reshape(1, -1),
        routes,
    )
    return received.reshape(1, pool_size, most, BLOCK, local_heads, width)


def solution(mesh):
    placed = (P(("groups", "pool"), "tp"), P("tp", None, None), P("groups"), P("groups", None))
    return jax.shard_map(
        functools.partial(on_device, mesh.shape["pool"], mesh.shape["tp"]),
        mesh=mesh,
        in_specs=placed,
        out_specs=P(("groups", "pool"), None, None, None, "tp", None),
        check_vma=False,
    )
```

time: 105 us -> 37.1 us (0.35)
  waiting for transfers between devices: 66.9 us -> 0 us
  Pallas kernels: 0 us -> 27.8 us
  between operations: 13.5 us -> 0.07 us
  local copies, waits for them, and re-layouts: 12.8 us -> 2.99 us
  other arithmetic: 3.42 us -> 0.1 us
  matrix products: 8.24 us -> 5.95 us
    reduce_scatter x1 -> x0, waiting for transfers between devices: 35.8 us -> none  [on_device(): lax.psum_scatter(jnp.einsum('td,dkc->ktc', tokens, w_kv, preferred_elemen...]
    all_gather x1 -> x0, waiting for transfers between devices: 31 us -> none  [on_device(): every_page = lax.all_gather(pages, 'pool', axis=0, tiled=True)]
    pallas_call x0 -> x1, Pallas kernels: none -> 27.8 us  [on_device(): pl.pallas_call(functools.partial(hand_over, pool_size, tp_size, most), ou...]
    all_gather x1 -> x0, local copies, waits for them, and re-layouts: 3.67 us -> none  [on_device(): every_page = lax.all_gather(pages, 'pool', axis=0, tiled=True)]
    reshape x2 -> x1, local copies, waits for them, and re-layouts: 3.46 us -> 1.38 us  [on_device(): return received.reshape(1, pool_size, most, BLOCK, local_heads, width)]
    dot_general x1, matrix products: 7.78 us -> 5.95 us  [on_device(): jnp.einsum('td,dkc->ktc', tokens, w_kv, preferred_element_type=jnp.float32)]
    concatenate x2 -> x0, local copies, waits for them, and re-layouts: 1.74 us -> none  [on_device(): jnp.concatenate([rotated, kv_rows[..., head_dim:]], axis=-1)]
    unnamed x7, local copies, waits for them, and re-layouts: 2.44 us -> 0.8 us
  transfers between devices with their start and end apart: 2 -> 0, of which waited for: 2 -> 0; matrix products, arithmetic and copies ran while one was open for 3% -> 0% of each run, Pallas kernels for 0% -> 0%
where the time goes in v1:
time: 37.1 us; the launch traced here: 36.9 us
  Pallas kernels  27.8 us (75%)
  matrix products  5.95 us (16%)
  local copies, waits for them, and re-layouts  2.99 us (8%)
    pallas_call x1, Pallas kernels, on_device(): pl.pallas_call(functools.partial(hand_over, pool_size, tp_size, most), ou...  27.8 us
    dot_general x1, matrix products, on_device(): jnp.einsum('td,dkc->ktc', tokens, w_kv, preferred_element_type=jnp.float32)  5.95 us
    reshape x1, local copies, waits for them, and re-layouts, on_device(): return received.reshape(1, pool_size, most, BLOCK, local_heads, width)  1.38 us
    broadcast_in_dim x1, local copies, waits for them, and re-layouts, on_device(): prompt_lens[:, None]  0.82 us
    unnamed x7, local copies, waits for them, and re-layouts  0.8 us

profile of v1, /device:TPU:0, one launch (start us, length us, event | category | flops | bytes accessed | tf_op | source)
XLA Modules:
  0.0 36.9 jit_solution(2265616482788551651)
XLA Ops:
  0.0 0.0 copy-start
  0.0 0.1 maximum_bitcast_fusion.freq_ref
  0.1 0.8 %copy.6.lens_col_ref = s32[16,1]{1,0:T(8,128)S(1)} copy(s32[16,1]{0,1:T(1,128)} %bitcast.13) | data formatting | bytes 128 | tf_op jit(solution)/shard_map/broadcast_in_dim | solution.py:223
  0.9 0.8 %copy.7.route_col_ref = s32[160,1]{1,0:T(8,128)S(1)} copy(s32[160,1]{0,1:T(1,128)} %param.7) | data formatting | bytes 1280 | tf_op args[3]
  1.7 0.0 copy-done
  1.7 0.0 copy-start.1
  1.7 0.0 copy-start.2
  1.7 6.0 %fusion.2.partial_ref = f32[8,320,256]{2,1,0:T(8,128)S(1)} fusion(bf16[2048,8,256]{2,1,0:T(8,128)(2,1)} %param.5, bf16[320,2048]{1,0:T(8,128)(2,1)S(1)} %copy-done), kind=kOutput, calls=%fused_computation.2 | convolution fusion | flops 2684354560 | bytes 12320768 | tf_op jit(solution)/shard_map/td,dkc->ktc/dot_general | solution.py:193
  7.7 0.0 copy-done.1
  7.7 0.0 copy-done.2
  7.7 27.8 %shard_map.46 = bf16[640,512]{1,0:T(8,128)(2,1)S(1)} custom-call(f32[8,320,256]{2,1,0:T(8,128)S(1)} %fusion.2.partial_ref, f32[1,128]{1,0:T(1,128)S(1)} %maximum_bitcast_fusion.freq_ref, s32[1,16]{1,0:T(1,128)S(1)} %bitcast.14, s32[16,1]{1,0:T(8,128)S(1)} %copy.6.lens_col_ref, s32[1,160]{1,0:T(1,128)S(1)} %bitcast.12, s32[160,1]{1,0:T(8,128)S(1)} %copy.7.route_col_ref), custom_call_target="tpu_custom_call" | custom-call | tf_op jit(solution)/shard_map/pallas_call | solution.py:198
  35.6 1.4 %copy.8 = bf16[1,4,20,8,2,256]{5,4,3,2,1,0:T(2,128)(2,1)} copy(bf16[1,4,20,8,2,256]{5,3,4,2,1,0:T(8,128)(2,1)S(1)} %bitcast.11) | data formatting | bytes 1310720 | tf_op jit(solution)/shard_map/reshape | solution.py:227
  (1 shorter events, 0.0 us)
Async XLA Ops:
  0.0 1.7 %copy-start = (bf16[320,2048]{1,0:T(8,128)(2,1)S(1)}, bf16[320,2048]{1,0:T(8,128)(2,1)}, u32[]{:S(2)}) copy-start(bf16[320,2048]{1,0:T(8,128)(2,1)} %param.4) | copy-start | bytes 3932164
  1.7 6.0 %copy-start.1 = (s32[160,1]{0,1:T(1,128)S(1)}, s32[160,1]{0,1:T(1,128)}, u32[]{:S(2)}) copy-start(s32[160,1]{0,1:T(1,128)} %param.7) | copy-start | bytes 1924
  1.7 6.0 %copy-start.2 = (s32[16]{0:T(128)S(1)}, s32[16]{0:T(128)}, u32[]{:S(2)}) copy-start(s32[16]{0:T(128)} %param.6) | copy-start | bytes 196

commit v2 on v1

--- a/solution.py
+++ b/solution.py
@@ -10,6 +10,7 @@
 
 BLOCK = 8
 LANES = 128
+DEPTH = 256
 MESH = pl.DeviceIdType.MESH
 
 
@@ -26,22 +27,36 @@
 
 def hand_over(
     pool_size, tp_size, most,
-    partial_ref, freq_ref, lens_row_ref, lens_col_ref, route_row_ref, route_col_ref,
+    tokens_hbm, w_hbm, freq_ref, lens_ref, route_ref,
     out_ref,
+    tokens, w_in, w_heads, partial,
     pair_in, across_out, across_in, placed, select, cosine, sine,
-    pair_sems, across_sems, pool_sems, local_sems,
+    in_sems, pair_sems, across_sems, pool_sems, local_sems,
 ):
     pool_index = lax.axis_index("pool")
     tp_index = lax.axis_index("tp")
     chip, core = tp_index // 2, tp_index % 2
     chips = tp_size // 2
-    rows = partial_ref.shape[1]
-    local_heads = partial_ref.shape[0] // tp_size
-    parts = partial_ref.shape[2] // LANES
+    rows = tokens.shape[0]
+    local_heads = partial.shape[0] // tp_size
+    parts = partial.shape[2] // LANES
     chunks = [(j, part) for j in range(local_heads) for part in range(parts)]
     span = most * BLOCK
     page_count = rows // BLOCK
     slot_rows = pool_size * span
+
+    tokens_in = pltpu.make_async_copy(tokens_hbm, tokens, in_sems.at[0])
+    depth = min(DEPTH, w_in.shape[0])
+    steps = w_in.shape[0] // depth
+    w_copies = [
+        pltpu.make_async_copy(
+            w_hbm.at[pl.ds(i * depth, depth)], w_in.at[pl.ds(i * depth, depth)], in_sems.at[i + 1]
+        )
+        for i in range(steps)
+    ]
+    for copy in w_copies:
+        copy.start()
+    tokens_in.start()
 
     def head_of(chip_of, core_of, j):
         return (chip_of * 2 + core_of) * local_heads + j
@@ -52,10 +67,18 @@
     peers += [{"pool": lax.rem(pool_index + d, pool_size)} for d in range(1, pool_size)]
     for peer in peers:
         pl.semaphore_signal(barrier, inc=1, device_id=peer, device_id_type=MESH)
-    pl.semaphore_wait(barrier, len(peers))
+
+    for i, copy in enumerate(w_copies):
+        copy.wait()
+        block = slice(i * depth, (i + 1) * depth)
+        w_heads[:, block, :] = jnp.swapaxes(w_in[block], 0, 1)
+    tokens_in.wait()
+
+    def multiply(head):
+        partial[head] = jnp.dot(tokens[...], w_heads[head], preferred_element_type=jnp.float32)
 
     def window(head, part):
-        return partial_ref.at[head, :, pl.ds(part * LANES, LANES)]
+        return partial.at[head, :, pl.ds(part * LANES, LANES)]
 
     def pair_copy(n, d):
         j, part = chunks[n]
@@ -97,55 +120,64 @@
             placed.at[n, block], out_ref.at[block, pl.ds(n * LANES, LANES)], local_sems.at[n]
         )
 
-    hops = [d % chips for d in range(1, chips + 1)]
-    for n in range(len(chunks)):
-        for d in hops:
-            pair_copy(n, d).start()
-    for n, (j, part) in enumerate(chunks):
-        for d in range(1, chips):
+    def to_pair(j, d):
+        multiply(head_of(lax.rem(chip + d, chips), 1 - core, j))
+        for part in range(parts):
+            pair_copy(j * parts + part, d).start()
+
+    def to_others(j, d):
+        for part in range(parts):
+            n = j * parts + part
             pair_copy(n, d).wait_recv()
             head = head_of(lax.rem(chip + d, chips), core, j)
             across_out[n, d - 1] = (
-                partial_ref[head, :, part * LANES:(part + 1) * LANES] + pair_in[n, d]
+                partial[head, :, part * LANES:(part + 1) * LANES] + pair_in[n, d]
             )
             across_copy(n, d).start()
 
+    pl.semaphore_wait(barrier, len(peers))
+    others = [(j, d) for j in range(local_heads) for d in range(1, chips)]
+    to_pair(*others[0])
+    multiply(head_of(lax.rem(chip + others[0][1], chips), core, others[0][0]))
+    for j, d in others[1:]:
+        to_pair(j, d)
+    for j in range(local_heads):
+        to_pair(j, 0)
+    to_others(*others[0])
+    for j, d in others[1:]:
+        multiply(head_of(lax.rem(chip + d, chips), core, j))
+        to_others(j, d)
+    for j in range(local_heads):
+        multiply(head_of(chip, core, j))
+
     def iota(shape, axis):
         return lax.broadcasted_iota(jnp.int32, shape, axis)
 
-    prompts = lens_row_ref.shape[1]
-    upto = iota((prompts, prompts), 0) <= iota((prompts, prompts), 1)
-    ends = jnp.sum(jnp.where(upto, lens_col_ref[...].astype(jnp.float32), 0.0), axis=0, keepdims=True)
+    def turned_row(column):
+        count = column.shape[0]
+        same = iota((count, count), 0) == iota((count, count), 1)
+        return jnp.sum(jnp.where(same, column, 0.0), axis=0, keepdims=True)
+
+    prompts = lens_ref.shape[1]
+    lens = lens_ref[...].astype(jnp.float32)
+    upto = iota((prompts, prompts), 1) <= iota((prompts, prompts), 0)
+    ends = turned_row(jnp.sum(jnp.where(upto, lens, 0.0), axis=1, keepdims=True))
     token = (pool_index * rows + iota((rows, prompts), 0)).astype(jnp.float32)
-    before = jnp.sum(
-        jnp.where(ends <= token, lens_row_ref[...].astype(jnp.float32), 0.0), axis=1, keepdims=True
-    )
+    before = jnp.sum(jnp.where(ends <= token, lens, 0.0), axis=1, keepdims=True)
     position = token[:, :1] - before
     angle = position * freq_ref[...]
     cosine[...] = jnp.cos(angle)
     turned = jnp.sin(angle)
     sine[...] = jnp.where(iota((rows, LANES), 1) < LANES // 2, -turned, turned)
 
-    pages = route_row_ref.shape[1]
-    first = pool_index * page_count
-    target_row = jnp.sum(
-        jnp.where(
-            iota((pages, rows), 0) == first + (iota((pages, rows), 1) >> 3),
-            route_col_ref[...].astype(jnp.float32),
-            0.0,
-        ),
-        axis=0,
-        keepdims=True,
-    )
+    pages = route_ref.shape[1]
+    own_page = pool_index * page_count + (iota((rows, pages), 0) >> 3)
     target_col = jnp.sum(
-        jnp.where(
-            iota((rows, pages), 1) == first + (iota((rows, pages), 0) >> 3),
-            route_row_ref[...].astype(jnp.float32),
-            0.0,
-        ),
+        jnp.where(iota((rows, pages), 1) == own_page, route_ref[...].astype(jnp.float32), 0.0),
         axis=1,
         keepdims=True,
     )
+    target_row = turned_row(target_col)
     earlier = (iota((rows, rows), 0) >> 3) < (iota((rows, rows), 1) >> 3)
     rank = jnp.sum(
         jnp.where(earlier & (target_col == target_row), 1.0, 0.0), axis=0, keepdims=True
@@ -157,9 +189,7 @@
 
     for n, (j, part) in enumerate(chunks):
         pair_copy(n, 0).wait_recv()
-        total = (
-            partial_ref[head_of(chip, core, j), :, part * LANES:(part + 1) * LANES] + pair_in[n, 0]
-        )
+        total = partial[head_of(chip, core, j), :, part * LANES:(part + 1) * LANES] + pair_in[n, 0]
         for d in range(1, chips):
             across_copy(n, d).wait_recv()
             total = total + across_in[n, d - 1]
@@ -186,21 +216,26 @@
 
 def on_device(pool_size, tp_size, tokens, w_kv, prompt_lens, routes):
     rows = tokens.shape[0]
-    heads, width = w_kv.shape[1:]
+    features, heads, width = w_kv.shape
     local_heads = heads // tp_size
     most = max(2, 2 * (rows // BLOCK) // pool_size)
     slot_rows = pool_size * most * BLOCK
-    partial = jnp.einsum("td,dkc->ktc", tokens, w_kv, preferred_element_type=jnp.float32)
     freqs = frequencies(width // 2)
     chunks = local_heads * width // LANES
     chips = tp_size // 2
+    steps = max(1, features // DEPTH)
     vmem = pl.BlockSpec(memory_space=pltpu.VMEM)
+    hbm = pl.BlockSpec(memory_space=pl.ANY)
     received = pl.pallas_call(
         functools.partial(hand_over, pool_size, tp_size, most),
         out_shape=jax.ShapeDtypeStruct((slot_rows, local_heads * width), jnp.bfloat16),
-        in_specs=[vmem] * 6,
+        in_specs=[hbm, hbm, vmem, vmem, vmem],
         out_specs=vmem,
         scratch_shapes=[
+            pltpu.VMEM(tokens.shape, jnp.bfloat16),
+            pltpu.VMEM(w_kv.shape, jnp.bfloat16),
+            pltpu.VMEM((heads, features, width), jnp.bfloat16),
+            pltpu.VMEM((heads, rows, width), jnp.float32),
             pltpu.VMEM((chunks, chips, rows, LANES), jnp.float32),
             pltpu.VMEM((chunks, chips - 1, rows, LANES), jnp.float32),
             pltpu.VMEM((chunks, chips - 1, rows, LANES), jnp.float32),
@@ -208,21 +243,21 @@
             pltpu.VMEM((slot_rows, rows), jnp.bfloat16),
             pltpu.VMEM((rows, LANES), jnp.float32),
             pltpu.VMEM((rows, LANES), jnp.float32),
+            pltpu.SemaphoreType.DMA((steps + 1,)),
             pltpu.SemaphoreType.DMA((2, chunks, chips)),
             pltpu.SemaphoreType.DMA((2, chunks, chips - 1)),
             pltpu.SemaphoreType.DMA((2, chunks, pool_size - 1)),
             pltpu.SemaphoreType.DMA((chunks,)),
         ],
         compiler_params=pltpu.CompilerParams(
-            collective_id=0, has_side_effects=True, vmem_limit_bytes=40 * 2**20
+            collective_id=0, has_side_effects=True, vmem_limit_bytes=56 * 2**20
         ),
     )(
-        partial,
+        tokens,
+        w_kv,
         jnp.concatenate([freqs, freqs])[None, :],
         prompt_lens[None, :],
-        prompt_lens[:, None],
         routes.reshape(1, -1),
-        routes,
     )
     return received.reshape(1, pool_size, most, BLOCK, local_heads, width)
 

time: 37.1 us -> 37 us (level)
  matrix products: 5.95 us -> 0 us
  Pallas kernels: 27.8 us -> 33.7 us
  local copies, waits for them, and re-layouts: 2.99 us -> 2.46 us
  other arithmetic: 0.1 us -> 0.61 us
    dot_general x1 -> x0, matrix products: 5.95 us -> none  [on_device(): jnp.einsum('td,dkc->ktc', tokens, w_kv, preferred_element_type=jnp.float32)]
    pallas_call x1, Pallas kernels: 27.8 us -> 33.7 us  [on_device(): pl.pallas_call(functools.partial(hand_over, pool_size, tp_size, most), ou...]
    reshape x1, local copies, waits for them, and re-layouts: 1.38 us -> 2.46 us  [on_device(): return received.reshape(1, pool_size, most, BLOCK, local_heads, width)]
    broadcast_in_dim x1 -> x0, local copies, waits for them, and re-layouts: 0.82 us -> none  [on_device(): prompt_lens[:, None]]
    unnamed x7 -> x0, local copies, waits for them, and re-layouts: 0.8 us -> none
    broadcast_in_dim x1, other arithmetic: 0.08 us -> 0.59 us  [on_device(): jnp.concatenate([freqs, freqs])[None, :]]
where the time goes in v2:
time: 37 us; the launch traced here: 36.8 us
  Pallas kernels  33.7 us (91%)
  local copies, waits for them, and re-layouts  2.46 us (7%)
  other arithmetic  0.61 us (2%)
    pallas_call x1, Pallas kernels, on_device(): pl.pallas_call(functools.partial(hand_over, pool_size, tp_size, most), ou...  33.7 us
    reshape x1, local copies, waits for them, and re-layouts, on_device(): return received.reshape(1, pool_size, most, BLOCK, local_heads, width)  2.46 us

profile of v2, /device:TPU:0, one launch (start us, length us, event | category | flops | bytes accessed | tf_op | source)
XLA Modules:
  0.0 36.8 jit_solution(12590792549075408770)
XLA Ops:
  0.0 0.6 %maximum_bitcast_fusion.freq_ref = f32[1,128]{1,0:T(1,128)} fusion(f32[64]{0:T(128)S(1)} %compare_select_fusion.1), kind=kLoop, calls=%fused_computation.2 | loop fusion | flops 128 | bytes 768 | tf_op jit(solution)/shard_map/broadcast_in_dim | solution.py:258
  0.6 33.7 %shard_map.46 = bf16[640,512]{1,0:T(8,128)(2,1)} custom-call(bf16[320,2048]{1,0:T(8,128)(2,1)} %tokens_hbm.1, bf16[2048,8,256]{2,1,0:T(8,128)(2,1)} %w_hbm.1, f32[1,128]{1,0:T(1,128)} %maximum_bitcast_fusion.freq_ref, s32[1,16]{1,0:T(1,128)} %bitcast.7, s32[1,160]{1,0:T(1,128)} %bitcast.6), custom_call_target="tpu_custom_call" | custom-call | tf_op jit(solution)/shard_map/pallas_call | solution.py:229
  34.3 2.5 %copy.5 = bf16[1,4,20,8,2,256]{5,4,3,2,1,0:T(2,128)(2,1)} copy(bf16[1,4,20,8,2,256]{5,3,4,2,1,0:T(8,128)(2,1)} %bitcast.5) | data formatting | bytes 1310720 | tf_op jit(solution)/shard_map/reshape | solution.py:262
  (1 shorter events, 0.0 us)

commit v3 on v2

--- a/solution.py
+++ b/solution.py
@@ -11,6 +11,7 @@
 BLOCK = 8
 LANES = 128
 DEPTH = 256
+EARLY = 4
 MESH = pl.DeviceIdType.MESH
 
 
@@ -54,9 +55,9 @@
         )
         for i in range(steps)
     ]
+    tokens_in.start()
     for copy in w_copies:
         copy.start()
-    tokens_in.start()
 
     def head_of(chip_of, core_of, j):
         return (chip_of * 2 + core_of) * local_heads + j
@@ -68,11 +69,25 @@
     for peer in peers:
         pl.semaphore_signal(barrier, inc=1, device_id=peer, device_id_type=MESH)
 
+    def head_for(d, core_of, j):
+        return head_of(lax.rem(chip + d, chips), core_of, j)
+
+    early = [
+        head_for(d, side, j)
+        for j in range(local_heads)
+        for d in range(1, chips)
+        for side in (1 - core, core)
+    ][:EARLY]
+    tokens_in.wait()
     for i, copy in enumerate(w_copies):
         copy.wait()
         block = slice(i * depth, (i + 1) * depth)
         w_heads[:, block, :] = jnp.swapaxes(w_in[block], 0, 1)
-    tokens_in.wait()
+        for head in early:
+            product = jnp.dot(
+                tokens[:, block], w_heads[head, block, :], preferred_element_type=jnp.float32
+            )
+            partial[head] = product if i == 0 else partial[head] + product
 
     def multiply(head):
         partial[head] = jnp.dot(tokens[...], w_heads[head], preferred_element_type=jnp.float32)
@@ -120,8 +135,9 @@
             placed.at[n, block], out_ref.at[block, pl.ds(n * LANES, LANES)], local_sems.at[n]
         )
 
-    def to_pair(j, d):
-        multiply(head_of(lax.rem(chip + d, chips), 1 - core, j))
+    def to_pair(j, d, ready):
+        if not ready:
+            multiply(head_for(d, 1 - core, j))
         for part in range(parts):
             pair_copy(j * parts + part, d).start()
 
@@ -137,16 +153,16 @@
 
     pl.semaphore_wait(barrier, len(peers))
     others = [(j, d) for j in range(local_heads) for d in range(1, chips)]
-    to_pair(*others[0])
-    multiply(head_of(lax.rem(chip + others[0][1], chips), core, others[0][0]))
-    for j, d in others[1:]:
-        to_pair(j, d)
-    for j in range(local_heads):
-        to_pair(j, 0)
-    to_others(*others[0])
-    for j, d in others[1:]:
-        multiply(head_of(lax.rem(chip + d, chips), core, j))
+    done = len(early) // 2
+    for k, (j, d) in enumerate(others):
+        to_pair(j, d, k < done)
+    to_pair(0, 0, False)
+    for k, (j, d) in enumerate(others):
+        if k >= done:
+            multiply(head_for(d, core, j))
         to_others(j, d)
+    for j in range(1, local_heads):
+        to_pair(j, 0, False)
     for j in range(local_heads):
         multiply(head_of(chip, core, j))
 
@@ -225,7 +241,7 @@
     chips = tp_size // 2
     steps = max(1, features // DEPTH)
     vmem = pl.BlockSpec(memory_space=pltpu.VMEM)
-    hbm = pl.BlockSpec(memory_space=pl.ANY)
+    hbm = pl.BlockSpec(memory_space=pltpu.HBM)
     received = pl.pallas_call(
         functools.partial(hand_over, pool_size, tp_size, most),
         out_shape=jax.ShapeDtypeStruct((slot_rows, local_heads * width), jnp.bfloat16),
@@ -250,7 +266,7 @@
             pltpu.SemaphoreType.DMA((chunks,)),
         ],
         compiler_params=pltpu.CompilerParams(
-            collective_id=0, has_side_effects=True, vmem_limit_bytes=56 * 2**20
+            collective_id=0, has_side_effects=True, vmem_limit_bytes=53 * 2**20
         ),
     )(
         tokens,

time: 37 us -> 35.9 us (0.970)
  Pallas kernels: 33.7 us -> 32.9 us
  other arithmetic: 0.61 us -> 0.1 us
    unnamed x0 -> x4, local copies, waits for them, and re-layouts: none -> 1.34 us
    reshape x1, local copies, waits for them, and re-layouts: 2.46 us -> 1.38 us  [on_device(): return received.reshape(1, pool_size, most, BLOCK, local_heads, width)]
    pallas_call x1, Pallas kernels: 33.7 us -> 32.9 us  [on_device(): pl.pallas_call(functools.partial(hand_over, pool_size, tp_size, most), ou...]
    broadcast_in_dim x1, other arithmetic: 0.59 us -> 0.08 us  [on_device(): jnp.concatenate([freqs, freqs])[None, :]]
where the time goes in v3:
time: 35.9 us; the launch traced here: 35.7 us
  Pallas kernels  32.9 us (92%)
  local copies, waits for them, and re-layouts  2.71 us (8%)
    pallas_call x1, Pallas kernels, on_device(): pl.pallas_call(functools.partial(hand_over, pool_size, tp_size, most), ou...  32.9 us
    reshape x1, local copies, waits for them, and re-layouts, on_device(): return received.reshape(1, pool_size, most, BLOCK, local_heads, width)  1.38 us
    unnamed x4, local copies, waits for them, and re-layouts  1.34 us

profile of v3, /device:TPU:0, one launch (start us, length us, event | category | flops | bytes accessed | tf_op | source)
XLA Modules:
  0.0 35.7 jit_solution(3560168638034186713)
XLA Ops:
  0.0 0.1 maximum_bitcast_fusion.freq_ref
  0.1 0.0 copy-start
  0.1 0.7 %copy-done = s32[160,1]{0,1:T(1,128)S(1)} copy-done((s32[160,1]{0,1:T(1,128)S(1)}, s32[160,1]{0,1:T(1,128)}, u32[]{:S(2)}) %copy-start) | copy-done | bytes 664
  0.8 0.0 copy-start.1
  0.8 0.7 %copy-done.1 = s32[16]{0:T(128)S(1)} copy-done((s32[16]{0:T(128)S(1)}, s32[16]{0:T(128)}, u32[]{:S(2)}) %copy-start.1) | copy-done | bytes 88
  1.4 32.9 %shard_map.46 = bf16[640,512]{1,0:T(8,128)(2,1)S(1)} custom-call(bf16[320,2048]{1,0:T(8,128)(2,1)} %tokens_hbm.1, bf16[2048,8,256]{2,1,0:T(8,128)(2,1)} %w_hbm.1, f32[1,128]{1,0:T(1,128)S(1)} %maximum_bitcast_fusion.freq_ref, s32[1,16]{1,0:T(1,128)S(1)} %bitcast.7, s32[1,160]{1,0:T(1,128)S(1)} %bitcast.6), custom_call_target="tpu_custom_call" | custom-call | tf_op jit(solution)/shard_map/pallas_call | solution.py:245
  34.3 1.4 %copy.5 = bf16[1,4,20,8,2,256]{5,4,3,2,1,0:T(2,128)(2,1)} copy(bf16[1,4,20,8,2,256]{5,3,4,2,1,0:T(8,128)(2,1)S(1)} %bitcast.5) | data formatting | bytes 1310720 | tf_op jit(solution)/shard_map/reshape | solution.py:278
  (1 shorter events, 0.0 us)
Async XLA Ops:
  0.1 0.7 %copy-start = (s32[160,1]{0,1:T(1,128)S(1)}, s32[160,1]{0,1:T(1,128)}, u32[]{:S(2)}) copy-start(s32[160,1]{0,1:T(1,128)} %param.7) | copy-start | bytes 1924
  0.8 0.7 %copy-start.1 = (s32[16]{0:T(128)S(1)}, s32[16]{0:T(128)}, u32[]{:S(2)}) copy-start(s32[16]{0:T(128)} %param.6) | copy-start | bytes 196

commit v4 on v3

--- a/solution.py
+++ b/solution.py
@@ -149,7 +149,8 @@
             across_out[n, d - 1] = (
                 partial[head, :, part * LANES:(part + 1) * LANES] + pair_in[n, d]
             )
-            across_copy(n, d).start()
+            if n == 0:
+                across_copy(n, d).start()
 
     pl.semaphore_wait(barrier, len(peers))
     others = [(j, d) for j in range(local_heads) for d in range(1, chips)]
@@ -165,6 +166,9 @@
         to_pair(j, 0, False)
     for j in range(local_heads):
         multiply(head_of(chip, core, j))
+    for n in range(1, min(2, len(chunks))):
+        for d in range(1, chips):
+            across_copy(n, d).start()
 
     def iota(shape, axis):
         return lax.broadcasted_iota(jnp.int32, shape, axis)
@@ -209,6 +213,8 @@
         for d in range(1, chips):
             across_copy(n, d).wait_recv()
             total = total + across_in[n, d - 1]
+            if n + 2 < len(chunks):
+                across_copy(n + 2, d).start()
         if part == 0:
             half = LANES // 2
             swapped = jnp.concatenate([total[:, half:], total[:, :half]], axis=1)

time: 35.9 us -> 35.9 us (level)
  no operation moved by 1% of the time
where the time goes in v4:
time: 35.9 us; the launch traced here: 35.7 us
  Pallas kernels  32.9 us (92%)
  local copies, waits for them, and re-layouts  2.71 us (8%)
    pallas_call x1, Pallas kernels, on_device(): pl.pallas_call(functools.partial(hand_over, pool_size, tp_size, most), ou...  32.9 us
    reshape x1, local copies, waits for them, and re-layouts, on_device(): return received.reshape(1, pool_size, most, BLOCK, local_heads, width)  1.38 us
    unnamed x4, local copies, waits for them, and re-layouts  1.34 us

profile of v4, /device:TPU:0, one launch (start us, length us, event | category | flops | bytes accessed | tf_op | source)
XLA Modules:
  0.0 35.7 jit_solution(1048999220797792222)
XLA Ops:
  0.0 0.1 maximum_bitcast_fusion.freq_ref
  0.1 0.0 copy-start
  0.1 0.7 %copy-done = s32[160,1]{0,1:T(1,128)S(1)} copy-done((s32[160,1]{0,1:T(1,128)S(1)}, s32[160,1]{0,1:T(1,128)}, u32[]{:S(2)}) %copy-start) | copy-done | bytes 664
  0.8 0.0 copy-start.1
  0.8 0.7 %copy-done.1 = s32[16]{0:T(128)S(1)} copy-done((s32[16]{0:T(128)S(1)}, s32[16]{0:T(128)}, u32[]{:S(2)}) %copy-start.1) | copy-done | bytes 88
  1.4 32.9 %shard_map.46 = bf16[640,512]{1,0:T(8,128)(2,1)S(1)} custom-call(bf16[320,2048]{1,0:T(8,128)(2,1)} %tokens_hbm.1, bf16[2048,8,256]{2,1,0:T(8,128)(2,1)} %w_hbm.1, f32[1,128]{1,0:T(1,128)S(1)} %maximum_bitcast_fusion.freq_ref, s32[1,16]{1,0:T(1,128)S(1)} %bitcast.7, s32[1,160]{1,0:T(1,128)S(1)} %bitcast.6), custom_call_target="tpu_custom_call" | custom-call | tf_op jit(solution)/shard_map/pallas_call | solution.py:251
  34.3 1.4 %copy.5 = bf16[1,4,20,8,2,256]{5,4,3,2,1,0:T(2,128)(2,1)} copy(bf16[1,4,20,8,2,256]{5,3,4,2,1,0:T(8,128)(2,1)S(1)} %bitcast.5) | data formatting | bytes 1310720 | tf_op jit(solution)/shard_map/reshape | solution.py:284
  (1 shorter events, 0.0 us)
Async XLA Ops:
  0.1 0.7 %copy-start = (s32[160,1]{0,1:T(1,128)S(1)}, s32[160,1]{0,1:T(1,128)}, u32[]{:S(2)}) copy-start(s32[160,1]{0,1:T(1,128)} %param.7) | copy-start | bytes 1924
  0.8 0.7 %copy-start.1 = (s32[16]{0:T(128)S(1)}, s32[16]{0:T(128)}, u32[]{:S(2)}) copy-start(s32[16]{0:T(128)} %param.6) | copy-start | bytes 196
